TPU v7x, 256 devices: a whole 4x4x8 slice. The times are simulated.
256 devices in a mesh: fsdp: 32 (over z, x), rep: 2 (over y_lo), tp: 4 (over y_hi, core).
Axes of the slice: x: 4, y: 4 (y_hi: 2, y_lo: 2; y = y_hi * 2 + y_lo), z: 8, core: 2. Of those that a mesh axis runs over, the one named last changes fastest.
Arguments:
- states: bfloat16 [4, 256, 5120], P(None, ('fsdp', 'rep')), may hold values from -6 to 6
- attn_gain: bfloat16 [5120], replicated, may hold values from 0.099609375 to 1.8984375
- w_qkv: float32 [5120, 5120], P('fsdp', ('rep', 'tp')), may hold values from -0.078125 to 0.078125
- w_out: float32 [4096, 5120], P(('rep', 'tp'), 'fsdp'), may hold values from -0.09375 to 0.09375
- q_gain: float32 [128], replicated, may hold values from 1 to 4
- k_gain: float32 [128], replicated, may hold values from 0.1 to 1.9
- k_cache: bfloat16 [256, 4, 2048, 128], P(('fsdp', 'rep'), 'tp'), may hold values from -110 to 110
- v_cache: bfloat16 [256, 4, 2048, 128], P(('fsdp', 'rep'), 'tp'), may hold values from -6 to 6
- lengths: int32 [256], P(('fsdp', 'rep')), may hold values from 1024 to 2048, as said below
Outputs:
- branch: bfloat16 [4, 256, 5120], P(None, ('fsdp', 'rep'))
Inputs may be any that keep to these rules, and one draw needn't show every extreme that they name: Sequence b holds cached positions 0 to lengths[b] - 1; its new token of step t stands at position lengths[b] + t.
All inputs are finite; a program needn't handle non-finite values.
Results may differ from a plain program's by a relative error of at most 0.015.
The roundings to bfloat16 on the way count: a program that leaves them out, or rounds other values in their place, can miss the bound.
Values may be sent and summed in bfloat16 or wider, within the bound.
A program may use at most 128 MiB of HBM per device.

v0:
```python
import math

import jax
import jax.numpy as jnp
from jax import lax
from jax.sharding import PartitionSpec as P

HQ = 32
HK = 4


EPSILON = 1e-06
THETA = 1000000.0


def normalize(values, gain):
    return values * lax.rsqrt(jnp.mean(values * values, axis=-1, keepdims=True) + EPSILON) * gain


def rotate(values, cosine, sine):
    half = values.shape[-1] // 2
    lower = values[..., :half]
    upper = values[..., half:]
    return jnp.concatenate([lower * cosine - upper * sine, upper * cosine + lower * sine], axis=-1)


def angles(lengths, steps, head):
    half = head // 2
    frequency = jnp.exp(jnp.arange(half, dtype=jnp.float32) * (-math.log(THETA) / half))
    position = (lengths[None, :] + jnp.arange(steps, dtype=jnp.int32)[:, None]).astype(jnp.float32)
    angle = position[:, :, None] * frequency
    return (jnp.cos(angle), jnp.sin(angle))


def attend(mixed, q_gain, k_gain, k_cache, v_cache, lengths, steps, seqs, groups, head):
    per_group = HQ // HK
    shaped = mixed.reshape(steps, seqs, groups, per_group + 2, head)
    cosine, sine = angles(lengths, steps, head)
    queries = rotate(
        normalize(shaped[..., :per_group, :], q_gain),
        cosine[:, :, None, None, :],
        sine[:, :, None, None, :],
    ).astype(jnp.bfloat16)
    keys = rotate(
        normalize(shaped[..., per_group, :], k_gain), cosine[:, :, None, :], sine[:, :, None, :]
    ).astype(jnp.bfloat16)
    values = shaped[..., per_group + 1, :].astype(jnp.bfloat16)
    scale = 1.0 / math.sqrt(head)
    slots = k_cache.shape[2]
    old_valid = (jnp.arange(slots, dtype=jnp.int32)[None, :] < lengths[:, None])[
        :, None, None, None, :
    ]
    step_mask = (
        jnp.arange(steps, dtype=jnp.int32)[None, :] <= jnp.arange(steps, dtype=jnp.int32)[:, None]
    )
    new_valid = step_mask[None, None, :, None, :]
    old_scores = (
        jnp.einsum("tsgqe,sgce->sgtqc", queries, k_cache, preferred_element_type=jnp.float32)
        * scale
    )
    new_scores = (
        jnp.einsum("tsgqe,usge->sgtqu", queries, keys, preferred_element_type=jnp.float32) * scale
    )
    highest = jnp.maximum(
        jnp.max(jnp.where(old_valid, old_scores, -1e30), axis=-1, keepdims=True),
        jnp.max(jnp.where(new_valid, new_scores, -1e30), axis=-1, keepdims=True),
    )
    old_exp = jnp.where(old_valid, jnp.exp(old_scores - highest), 0.0)
    new_exp = jnp.where(new_valid, jnp.exp(new_scores - highest), 0.0)
    total = jnp.sum(old_exp, axis=-1, keepdims=True) + jnp.sum(new_exp, axis=-1, keepdims=True)
    old_weight = (old_exp / total).astype(jnp.bfloat16)
    new_weight = (new_exp / total).astype(jnp.bfloat16)
    context = jnp.einsum(
        "sgtqc,sgce->tsgqe", old_weight, v_cache, preferred_element_type=jnp.float32
    )
    context = context + jnp.einsum(
        "sgtqu,usge->tsgqe", new_weight, values, preferred_element_type=jnp.float32
    )
    return context.astype(jnp.bfloat16).reshape(steps * seqs, groups * per_group * head)


def body(states, attn_gain, w_qkv, w_out, q_gain, k_gain, k_cache, v_cache, lengths):
    steps, seqs, width = states.shape
    groups = k_cache.shape[1]
    head = k_cache.shape[3]
    per_group = HQ // HK
    group_cols = (per_group + 2) * head
    group_rows = per_group * head
    tp_index = lax.axis_index("tp")
    half_in = w_qkv.astype(jnp.bfloat16)
    half_back = w_out.astype(jnp.bfloat16)
    all_in, all_back = (
        lax.all_gather(half_in, ("rep", "tp"), axis=1, tiled=True),
        lax.all_gather(half_back, ("rep", "tp"), axis=0, tiled=True),
    )
    own_in = lax.dynamic_slice_in_dim(
        all_in, tp_index * groups * group_cols, groups * group_cols, 1
    )
    own_back = lax.dynamic_slice_in_dim(
        all_back, tp_index * groups * group_rows, groups * group_rows, 0
    )
    rows = steps * seqs
    inputs = states.reshape(rows, width).astype(jnp.float32)
    normed = normalize(inputs, attn_gain.astype(jnp.float32)).astype(jnp.bfloat16)
    full_in, full_back = (
        lax.all_gather(own_in, "fsdp", axis=0, tiled=True),
        lax.all_gather(own_back, "fsdp", axis=1, tiled=True),
    )
    mixed = jnp.dot(normed, full_in, preferred_element_type=jnp.float32)
    context = attend(mixed, q_gain, k_gain, k_cache, v_cache, lengths, steps, seqs, groups, head)
    partial_out = jnp.dot(context, full_back, preferred_element_type=jnp.float32)
    summed = lax.psum(partial_out.astype(jnp.bfloat16), "tp")
    return summed.reshape(steps, seqs, width)


def solution(mesh):
    in_specs = (
        P(None, ("fsdp", "rep"), None),
        P(),
        P("fsdp", ("rep", "tp")),
        P(("rep", "tp"), "fsdp"),
        P(),
        P(),
        P(("fsdp", "rep"), "tp", None, None),
        P(("fsdp", "rep"), "tp", None, None),
        P(("fsdp", "rep")),
    )
    out_specs = P(None, ("fsdp", "rep"), None)
    return jax.shard_map(body, mesh=mesh, in_specs=in_specs, out_specs=out_specs, check_vma=False)
```

profile of v0, /device:TPU:1, one launch (start us, length us, event | category | flops | bytes accessed | tf_op | source)
XLA Modules:
  0.0 380.2 jit_solution(518723015297115790)
XLA Ops:
  6.5 0.0 copy-start
  6.5 0.0 all-gather.5.cloned.1.call-start
  6.6 1.9 convert_element_type.64
  8.4 0.0 all-gather.5.cloned.1.call-update
  8.5 0.0 all-gather.9.cloned.1.call-start
  8.5 1.7 convert_element_type.72
  10.2 0.0 all-gather.9.cloned.1.call-update
  10.2 0.0 all-gather.7.cloned.1.call-start
  10.3 39.6 %all-gather.5.cloned.1.call-done = bf16[160,5120]{1,0:T(8,128)(2,1)} async-done(((bf16[160,640]{1,0:T(8,128)(2,1)}), bf16[160,5120]{1,0:T(8,128)(2,1)}) %all-gather.5.cloned.1.call-update) | async-done | bytes 1638416 | tf_op jit(solution)/shard_map/all_gather | solution.py:93
  49.9 1.8 constant_dynamic-slice_fusion.1
  51.7 0.0 all-gather.7.cloned.1.call-update
  51.7 0.0 all-gather.11.cloned.1.call-start
  51.8 37.0 %all-gather.9.cloned.1.call-done = bf16[4096,160]{0,1:T(8,128)(2,1)} async-done(((bf16[512,160]{0,1:T(8,128)(2,1)}), bf16[4096,160]{0,1:T(8,128)(2,1)}) %all-gather.9.cloned.1.call-update) | async-done | bytes 1310736 | tf_op jit(solution)/shard_map/all_gather | solution.py:94
  88.8 1.7 constant_dynamic-slice_fusion
  90.5 0.0 all-gather.11.cloned.1.call-update
  90.5 0.0 all-reduce.2.cloned.1.call-start
  90.6 0.0 copy-done.2
  90.6 0.0 copy-done.1
  90.6 0.2 fusion.13
  90.8 0.0 copy-done.3
  90.8 0.1 multiply_cosine_fusion.1
  91.0 0.1 iota_compare_fusion
  91.1 121.2 %all-gather.7.cloned.1.call-done = bf16[5120,1280]{1,0:T(8,128)(2,1)} async-done(((bf16[160,1280]{1,0:T(8,128)(2,1)}), bf16[5120,1280]{1,0:T(8,128)(2,1)}) %all-gather.7.cloned.1.call-update) | async-done | bytes 13107216 | tf_op jit(solution)/shard_map/all_gather | solution.py:106
  212.3 17.7 %copy.15 = bf16[1280,5120]{1,0:T(8,128)(2,1)} copy(bf16[1280,5120]{0,1:T(8,128)(2,1)} %bitcast.61) | data formatting | bytes 26214400 | tf_op jit(solution)/shard_map/dot_general | solution.py:109
  230.0 6.8 %convolution_bitcast_fusion = f32[4,4,1,10,128]{4,1,3,0,2:T(4,128)S(1)} fusion(bf16[10,128,5120,1]{2,1,0,3:T(8,128)(2,1)} %bitcast.62, bf16[4,4,5120]{2,1,0:T(4,128)(2,1)S(1)} %copy-done.1, f32[5120]{0:T(1024)S(1)} %convert_element_type.62, f32[4,4]{1,0:T(4,128)S(1)} %add_rsqrt_fusion.2), kind=kOutput, calls=%fused_computation.5 | convolution fusion | flops 210042880 | bytes 13373504 | tf_op jit(solution)/shard_map/dot_general | solution.py:109
  236.8 0.1 multiply_reduce_fusion.1
  236.9 0.0 copy-done.5
  236.9 0.1 multiply_multiply_fusion.1
  237.0 0.1 fusion.43
  237.2 0.1 maximum_bitcast_fusion
  237.2 0.1 multiply_reduce_fusion
  237.4 0.1 multiply_multiply_fusion
  237.5 0.1 fusion.22
  237.6 0.1 pad_maximum_fusion
  237.7 0.3 select_reduce_fusion.1
  238.0 0.0 copy-start.6
  238.0 0.9 select_reduce_fusion
  238.9 0.1 fusion.26
  239.0 0.4 fusion.8
  239.4 0.2 copy-done.6
  239.6 0.5 fusion.3
  240.2 0.3 fusion.7
  240.4 80.4 %all-gather.11.cloned.1.call-done = bf16[1024,5120]{0,1:T(8,128)(2,1)} async-done(((bf16[1024,160]{0,1:T(8,128)(2,1)}), bf16[1024,5120]{0,1:T(8,128)(2,1)}) %all-gather.11.cloned.1.call-update) | async-done | bytes 10485776 | tf_op jit(solution)/shard_map/all_gather | solution.py:107
  320.9 6.8 %convolution_convert_fusion = bf16[16,5120]{1,0:T(8,128)(2,1)S(1)} fusion(bf16[1024,5120]{0,1:T(8,128)(2,1)} %all-gather.11.cloned.1.call-done, bf16[2,8,8,128]{3,2,1,0:T(8,128)(2,1)S(1)} %bitcast.63), kind=kOutput, calls=%fused_computation | convolution fusion | flops 167854080 | bytes 10682368 | tf_op jit(solution)/shard_map/dot_general | solution.py:111
  327.7 0.8 reshape.275
  328.4 0.0 all-reduce.2.cloned.1.call-update
  328.5 43.6 %all-reduce.2.cloned.1.call-done = bf16[4,4,5120]{2,1,0:T(4,128)(2,1)} async-done(((bf16[4,4,5120]{2,1,0:T(4,128)(2,1)}), bf16[4,4,5120]{2,1,0:T(4,128)(2,1)}) %all-reduce.2.cloned.1.call-update) | async-done | bytes 163856 | tf_op jit(solution)/shard_map/psum | solution.py:112
  372.0 1.6 copy.50
  (18 shorter events, 0.1 us)
Async XLA Ops:
  6.5 231.4 %copy-start = (bf16[4,1,2048,128]{3,2,1,0:T(8,128)(2,1)S(1)}, bf16[4,1,2048,128]{3,2,1,0:T(8,128)(2,1)}, u32[]{:S(2)}) copy-start(bf16[4,1,2048,128]{3,2,1,0:T(8,128)(2,1)} %param.15) | copy-start | bytes 6291460
  6.5 84.0 %copy-start.2 = (bf16[5120]{0:T(1024)(128)(2,1)S(1)}, bf16[5120]{0:T(1024)(128)(2,1)}, u32[]{:S(2)}) copy-start(bf16[5120]{0:T(1024)(128)(2,1)} %param.10) | copy-start | bytes 30724
  6.5 84.1 %copy-start.1 = (bf16[4,4,5120]{2,1,0:T(4,128)(2,1)S(1)}, bf16[4,4,5120]{2,1,0:T(4,128)(2,1)}, u32[]{:S(2)}) copy-start(bf16[4,4,5120]{2,1,0:T(4,128)(2,1)} %param.9) | copy-start | bytes 491524
  6.5 84.3 %copy-start.3 = (s32[4]{0:T(128)S(1)}, s32[4]{0:T(128)}, u32[]{:S(2)}) copy-start(s32[4]{0:T(128)} %param.17) | copy-start | bytes 52
  6.5 43.4 %all-gather.5.cloned.1.call-start = ((), (), s32[]{:S(2)}) async-start(), calls=%async_computation | async-start | bytes 1843200 | tf_op jit(solution)/shard_map/all_gather | solution.py:93
  8.5 80.3 %all-gather.9.cloned.1.call-start = ((), (), s32[]{:S(2)}) async-start(), calls=%async_computation.2 | async-start | bytes 1474560 | tf_op jit(solution)/shard_map/all_gather | solution.py:94
  10.2 202.1 %all-gather.7.cloned.1.call-start = ((), (), s32[]{:S(2)}) async-start(), calls=%async_computation.1 | async-start | bytes 13516800 | tf_op jit(solution)/shard_map/all_gather | solution.py:106
  51.7 269.2 %all-gather.11.cloned.1.call-start = ((), (), s32[]{:S(2)}) async-start(), calls=%async_computation.3 | async-start | bytes 10813440 | tf_op jit(solution)/shard_map/all_gather | solution.py:107
  90.5 281.5 %all-reduce.2.cloned.1.call-start = ((), (), s32[]{:S(2)}) async-start(), calls=%async_computation.4 | async-start | bytes 327680 | tf_op jit(solution)/shard_map/psum | solution.py:112
  230.0 6.9 %copy-start.5 = (f32[128]{0:T(128)S(1)}, f32[128]{0:T(128)}, u32[]{:S(2)}) copy-start(f32[128]{0:T(128)} %param.14) | copy-start | bytes 1540
  230.0 7.3 %copy-start.4 = (f32[128]{0:T(128)S(1)}, f32[128]{0:T(128)}, u32[]{:S(2)}) copy-start(f32[128]{0:T(128)} %param.13) | copy-start | bytes 1540
  238.0 1.6 copy-start.6
Sparse Core Ops, SparseCore 0:
  9.2 40.6 all-gather.4
  51.7 37.0 all-gather.8
  91.3 120.9 all-gather.6
  214.7 106.1 all-gather.10
  328.6 43.4 all-reduce.1
where the time goes:
time: 381 us; the launch traced here: 380 us
  waiting for transfers between devices  322 us (85%)
  local copies, waits for them, and re-layouts  23.9 us (6%)
  matrix products  15.5 us (4%)
  between operations  13.3 us (3%)
  other arithmetic  5.26 us (1%)
    all_gather x1, waiting for transfers between devices, body(): lax.all_gather(own_in, 'fsdp', axis=0, tiled=True)  121 us
    all_gather x1, waiting for transfers between devices, body(): lax.all_gather(own_back, 'fsdp', axis=1, tiled=True)  80.4 us
    psum x1, waiting for transfers between devices, body(): summed = lax.psum(partial_out.astype(jnp.bfloat16), 'tp')  43.6 us
    all_gather x1, waiting for transfers between devices, body(): lax.all_gather(half_in, ('rep', 'tp'), axis=1, tiled=True)  39.6 us
    all_gather x1, waiting for transfers between devices, body(): lax.all_gather(half_back, ('rep', 'tp'), axis=0, tiled=True)  37 us
    dot_general x1, local copies, waits for them, and re-layouts, body(): mixed = jnp.dot(normed, full_in, preferred_element_type=jnp.float32)  17.7 us
  transfers between devices with their start and end apart: 5, of which 5 were waited for; matrix products, arithmetic and copies ran while one was open for 9% of the time, Pallas kernels for 0%

commit v1 on v0

v1 whole, which is shorter than its diff:
```python
import functools
import math

import jax
import jax.numpy as jnp
import numpy as np
from jax import lax
from jax.experimental import pallas as pl
from jax.experimental.pallas import tpu as pltpu
from jax.sharding import PartitionSpec as P

MESH = pl.DeviceIdType.MESH
EPSILON = 1e-06
THETA = 1000000.0
NZ, NX = 8, 4
STEPS, SEQS, ROWS = 4, 4, 16
HEAD, SLOTS = 128, 10
IN_ROWS, IN_COLS = 160, 640
OUT_ROWS, OUT_COLS = 512, 160
CACHE, EXTRA = 2048, 128
KEYS = CACHE + EXTRA
BF, F32 = jnp.bfloat16, jnp.float32
SUM_TYPE = jnp.bfloat16


def kernel(
    states, attn_gain, w_qkv, w_out, q_gain, k_gain, frequency, lengths, k_cache, v_cache, out,
    kbuf, vbuf, xs, nbuf, abuf, wbuf, obuf, cbuf, crecv, mbuf, mrecv, qs, ks, cs, tbuf, xbuf, pbuf, rbuf, fbuf, gbuf, ybuf,
    local_sem, w_send, w_recv, o_send, o_recv, a_send, a_recv, b_send, b_recv, c_send, c_recv,
    m_send, m_recv, t_send, t_recv, x_send, x_recv, r_send, r_recv, g_send, g_recv, y_send, y_recv,
):
    f, yl, tp = lax.axis_index("fsdp"), lax.axis_index("rep"), lax.axis_index("tp")
    z, x, yh, c = f // NX, f % NX, tp // 2, tp % 2

    def at(pz, px, pl_, ph, pc):
        return (pz * NX + px, pl_, ph * 2 + pc)

    def send(src, dst, ssem, rsem, device):
        return pltpu.make_async_remote_copy(
            src_ref=src, dst_ref=dst, send_sem=ssem, recv_sem=rsem, device_id=device, device_id_type=MESH
        )

    def z_peer(k):
        return at((z + k) % NZ, x, yl, yh, c)

    def flip(d):
        return (
            1 - yl if d & 1 else yl,
            1 - yh if d & 2 else yh,
            1 - c if d & 4 else c,
        )

    right, left = at(z, (x + 1) % NX, yl, yh, c), at(z, (x + NX - 1) % NX, yl, yh, c)

    k_copy = pltpu.make_async_copy(k_cache.at[:, 0], kbuf.at[:, pl.ds(0, CACHE)], local_sem.at[0])
    v_copy = pltpu.make_async_copy(v_cache.at[:, 0], vbuf.at[:, pl.ds(0, CACHE)], local_sem.at[1])
    k_copy.start()
    v_copy.start()

    barrier = pltpu.get_barrier_semaphore()
    peers = [right, left]
    peers += [z_peer(k) for k in range(1, NZ)]
    peers += [at(z, x, *flip(d)) for d in range(1, 8)]
    for peer in peers:
        pl.semaphore_signal(barrier, inc=1, device_id=peer, device_id_type=MESH)

    wbuf[pl.ds(x, 1)] = w_qkv[...].astype(BF)[None]
    for s in range(STEPS):
        xs[pl.ds(s * SEQS, SEQS), :] = states[s].astype(F32)
    values = xs[...]
    mean = jnp.mean(values * values, axis=-1, keepdims=True)
    normed = (values * lax.rsqrt(mean + EPSILON) * attn_gain[...].astype(F32)).astype(BF)
    for k in range(NZ):
        nbuf[k] = normed[:, k * IN_COLS : (k + 1) * IN_COLS]
    abuf[0, 0] = nbuf[z]

    pl.semaphore_wait(barrier, len(peers))

    w_right = send(wbuf.at[x], wbuf.at[x], w_send.at[0], w_recv.at[0], right)
    w_left = send(wbuf.at[x], wbuf.at[x], w_send.at[1], w_recv.at[1], left)
    w_right.start()
    w_left.start()
    a_copies = []
    for k in range(1, NZ):
        copy = send(nbuf.at[(z + k) % NZ], abuf.at[0, k], a_send.at[k], a_recv.at[k], z_peer(k))
        copy.start()
        a_copies.append(copy)

    obuf[pl.ds(x, 1)] = jnp.transpose(w_out[...]).astype(BF)[None]
    row = lax.broadcasted_iota(jnp.int32, (ROWS, HEAD), 0)
    lane = lax.broadcasted_iota(jnp.int32, (ROWS, HEAD), 1)
    position = row // SEQS
    for b in range(SEQS):
        position = position + jnp.where(row % SEQS == b, lengths[b], 0)
    angle = position.astype(F32) * frequency[...]
    cosine = jnp.cos(angle)
    sine = jnp.where(lane < HEAD // 2, -jnp.sin(angle), jnp.sin(angle))
    for b in range(SEQS):
        kbuf[b, pl.ds(CACHE, EXTRA), :] = jnp.zeros((EXTRA, HEAD), BF)
        vbuf[b, pl.ds(CACHE, EXTRA), :] = jnp.zeros((EXTRA, HEAD), BF)

    for copy in a_copies:
        copy.wait_recv()
    half = NZ // 2
    b_copies = [
        send(abuf.at[0, pl.ds(0, half)], abuf.at[1, pl.ds(0, half)], b_send.at[0], b_recv.at[0], at(z, x, 1 - yl, yh, c)),
        send(abuf.at[0, pl.ds(half, half)], abuf.at[1, pl.ds(half, half)], b_send.at[1], b_recv.at[1], at(z, x, 1 - yl, 1 - yh, c)),
    ]
    for copy in b_copies:
        copy.start()

    from_left, from_right = (x + NX - 1) % NX, (x + 1) % NX
    part = IN_ROWS // 2
    w_right.wait_recv()
    w_on_right = send(
        wbuf.at[from_left, pl.ds(0, part)], wbuf.at[from_left, pl.ds(0, part)], w_send.at[2], w_recv.at[2], right
    )
    w_on_right.start()
    w_left.wait_recv()
    w_on_left = send(
        wbuf.at[from_right, pl.ds(part, part)], wbuf.at[from_right, pl.ds(part, part)], w_send.at[3], w_recv.at[3], left
    )
    w_on_left.start()
    w_on_right.wait_recv()
    w_on_left.wait_recv()
    for copy in b_copies:
        copy.wait_recv()

    weights = wbuf[...].reshape(NX * IN_ROWS, IN_COLS)
    for rel in range(2):
        rows = abuf[rel].reshape(NZ * ROWS, IN_COLS)
        mixed = jnp.dot(rows, weights, preferred_element_type=F32)
        cbuf[:, rel] = mixed.reshape(NZ, ROWS, IN_COLS).astype(SUM_TYPE)
    c_copies = []
    for k in range(1, NZ):
        copy = send(cbuf.at[NZ - k], crecv.at[k], c_send.at[k], c_recv.at[k], z_peer(k))
        copy.start()
        c_copies.append(copy)
    o_right = send(obuf.at[x], obuf.at[x], o_send.at[0], o_recv.at[0], right)
    o_left = send(obuf.at[x], obuf.at[x], o_send.at[1], o_recv.at[1], left)
    o_right.start()
    o_left.start()
    total = cbuf[0].astype(F32)
    for copy in c_copies:
        copy.wait_recv()
    for k in range(1, NZ):
        total = total + crecv[k].astype(F32)
    mbuf[...] = total

    is_self = jnp.logical_and(yl == yh, yh == c)
    m_first = send(mbuf.at[0], mrecv.at[c], m_send.at[0], m_recv.at[c], at(z, x, yl, yl, yh))
    m_second = send(mbuf.at[1], mrecv.at[c], m_send.at[1], m_recv.at[c], at(z, x, 1 - yl, yl, yh))
    m_second.start()

    @pl.when(jnp.logical_not(is_self))
    def _():
        m_first.start()

    @pl.when(is_self)
    def _():
        mrecv[pl.ds(c, 1)] = mbuf[0][None]

    o_right.wait_recv()
    o_on_right = send(
        obuf.at[from_left, pl.ds(0, part)], obuf.at[from_left, pl.ds(0, part)], o_send.at[2], o_recv.at[2], right
    )
    o_on_right.start()
    o_left.wait_recv()
    o_on_left = send(
        obuf.at[from_right, pl.ds(part, part)], obuf.at[from_right, pl.ds(part, part)], o_send.at[3], o_recv.at[3], left
    )
    o_on_left.start()
    for cc in range(2):

        @pl.when(jnp.logical_not(jnp.logical_and(is_self, c == cc)))
        def _():
            send(mbuf.at[0], mrecv.at[cc], m_send.at[0], m_recv.at[cc], right).wait_recv()

    def slot(j):
        at_half = SLOTS // 2
        return mrecv[j // at_half, :, pl.ds((j % at_half) * HEAD, HEAD)]

    def roped(v, gain):
        n = v * lax.rsqrt(jnp.mean(v * v, axis=-1, keepdims=True) + EPSILON) * gain
        return (n * cosine + pltpu.roll(n, HEAD // 2, 1) * sine).astype(BF).astype(F32)

    for j in range(SLOTS - 2):
        qs[pl.ds(j * ROWS, ROWS), :] = roped(slot(j), q_gain[...])
    ks[pl.ds(0, ROWS), :] = roped(slot(SLOTS - 2), k_gain[...])
    ks[pl.ds(ROWS, ROWS), :] = slot(SLOTS - 1)
    k_copy.wait()
    v_copy.wait()
    queries_of = STEPS * (SLOTS - 2)
    scale = 1.0 / math.sqrt(HEAD)
    column = lax.broadcasted_iota(jnp.int32, (queries_of, KEYS), 1)
    step = lax.broadcasted_iota(jnp.int32, (queries_of, KEYS), 0) % STEPS
    new_valid = jnp.logical_and(column >= CACHE, column - CACHE <= step)
    for b in range(SEQS):
        query = qs[pl.ds(b, queries_of, stride=SEQS), :].astype(BF)
        empty = jnp.zeros((ROWS - STEPS, HEAD), F32)
        kbuf[b, pl.ds(CACHE, ROWS), :] = jnp.concatenate([ks[pl.ds(b, STEPS, stride=SEQS), :], empty], axis=0).astype(BF)
        vbuf[b, pl.ds(CACHE, ROWS), :] = jnp.concatenate([ks[pl.ds(ROWS + b, STEPS, stride=SEQS), :], empty], axis=0).astype(BF)
        scores = lax.dot_general(query, kbuf[b], (((1,), (1,)), ((), ())), preferred_element_type=F32) * scale
        valid = jnp.logical_or(column < lengths[b], new_valid)
        highest = jnp.max(jnp.where(valid, scores, -1e30), axis=-1, keepdims=True)
        exps = jnp.where(valid, jnp.exp(scores - highest), 0.0)
        probs = (exps / jnp.sum(exps, axis=-1, keepdims=True)).astype(BF)
        cs[pl.ds(b, queries_of, stride=SEQS), :] = jnp.dot(probs, vbuf[b], preferred_element_type=F32)
    per_half = (SLOTS - 2) // 2
    for j in range(SLOTS - 2):
        tbuf[j // per_half, :, pl.ds((j % per_half) * HEAD, HEAD)] = cs[pl.ds(j * ROWS, ROWS), :].astype(BF)

    for cc in range(2):
        copy = send(tbuf.at[cc], xbuf.at[0, yl], t_send.at[cc], t_recv.at[yl], at(z, x, yh, c, cc))
        own = jnp.logical_and(is_self, c == cc)

        @pl.when(jnp.logical_not(own))
        def _():
            copy.start()

        @pl.when(own)
        def _():
            xbuf[0, pl.ds(yl, 1)] = tbuf[cc][None]

    for rr in range(2):

        @pl.when(jnp.logical_not(jnp.logical_and(is_self, yl == rr)))
        def _():
            send(tbuf.at[0], xbuf.at[0, rr], t_send.at[0], t_recv.at[rr], right).wait_recv()

    x_copies = []
    for k in range(1, NZ):
        copy = send(xbuf.at[0], xbuf.at[k], x_send.at[k], x_recv.at[k], z_peer(k))
        copy.start()
        x_copies.append(copy)
    o_on_right.wait_recv()
    o_on_left.wait_recv()
    for copy in x_copies:
        copy.wait_recv()
    contexts = xbuf[...].reshape(NZ * 2 * ROWS, OUT_ROWS)
    partial = lax.dot_general(
        contexts, obuf[...].reshape(NX * OUT_COLS, OUT_ROWS), (((1,), (1,)), ((), ())), preferred_element_type=F32
    )
    pbuf[...] = partial.reshape(NZ, 2, ROWS, NX * OUT_COLS).astype(BF)

    def ahead(pl_, ph, pc):
        return ph * 2 + pl_ + pc * 4

    r_copies = []
    for d in range(1, 8):
        peer = flip(d)
        copy = send(pbuf.at[(NZ - ahead(*peer)) % NZ], rbuf.at[d], r_send.at[d], r_recv.at[d], at(z, x, *peer))
        copy.start()
        r_copies.append(copy)
    mine = ahead(yl, yh, c)
    total = pbuf[(NZ - mine) % NZ].astype(F32)
    for copy in r_copies:
        copy.wait_recv()
    for d in range(1, 8):
        total = total + rbuf[d].astype(F32)
    fbuf[...] = total.astype(BF)

    g_copy = send(fbuf, gbuf, g_send.at[0], g_recv.at[0], at((z + mine) % NZ, x, yl, yh, c))

    @pl.when(mine != 0)
    def _():
        g_copy.start()
        g_copy.wait_recv()

    @pl.when(mine == 0)
    def _():
        gbuf[...] = fbuf[...]

    block = (z + NZ - mine) % NZ
    y_copies = []
    for d in range(1, 8):
        peer = flip(d)
        copy = send(gbuf.at[peer[0]], ybuf.at[block], y_send.at[d], y_recv.at[d], at(z, x, *peer))
        copy.start()
        y_copies.append(copy)
    ybuf[pl.ds(block, 1)] = gbuf[yl][None]
    for d in range(1, 8):
        theirs = (z + NZ - ahead(*flip(d))) % NZ
        send(gbuf.at[0], ybuf.at[theirs], y_send.at[d], y_recv.at[d], right).wait_recv()
    for k in range(NZ):
        block_rows = ybuf[k].astype(F32)
        for s in range(STEPS):
            out[s, :, pl.ds(k * IN_COLS, IN_COLS)] = block_rows[s * SEQS : (s + 1) * SEQS].astype(BF)

    for copy in [w_right, w_left, w_on_right, w_on_left, o_right, o_left, o_on_right, o_on_left, m_second]:
        copy.wait_send()
    for copy in a_copies + b_copies + c_copies + x_copies + r_copies + y_copies:
        copy.wait_send()

    @pl.when(jnp.logical_not(is_self))
    def _():
        m_first.wait_send()

    for cc in range(2):

        @pl.when(jnp.logical_not(jnp.logical_and(is_self, c == cc)))
        def _():
            send(tbuf.at[cc], xbuf.at[0, 0], t_send.at[cc], t_recv.at[0], right).wait_send()

    @pl.when(mine != 0)
    def _():
        g_copy.wait_send()


def body(states, attn_gain, w_qkv, w_out, q_gain, k_gain, k_cache, v_cache, lengths):
    half = HEAD // 2
    exponent = np.arange(half, dtype=np.float64) * (-math.log(THETA) / half)
    frequency = np.tile(np.exp(exponent).astype(np.float32), 2)[None]
    width = states.shape[2]
    vmem, hbm = pl.BlockSpec(memory_space=pltpu.VMEM), pl.BlockSpec(memory_space=pl.ANY)
    dma = pltpu.SemaphoreType.DMA
    return pl.pallas_call(
        kernel,
        out_shape=jax.ShapeDtypeStruct(states.shape, BF),
        in_specs=[vmem] * 7 + [pl.BlockSpec(memory_space=pltpu.SMEM), hbm, hbm],
        out_specs=vmem,
        scratch_shapes=[
            pltpu.VMEM((SEQS, KEYS, HEAD), BF),
            pltpu.VMEM((SEQS, KEYS, HEAD), BF),
            pltpu.VMEM((ROWS, width), F32),
            pltpu.VMEM((NZ, ROWS, IN_COLS), BF),
            pltpu.VMEM((2, NZ, ROWS, IN_COLS), BF),
            pltpu.VMEM((NX, IN_ROWS, IN_COLS), BF),
            pltpu.VMEM((NX, OUT_COLS, OUT_ROWS), BF),
            pltpu.VMEM((NZ, 2, ROWS, IN_COLS), SUM_TYPE),
            pltpu.VMEM((NZ, 2, ROWS, IN_COLS), SUM_TYPE),
            pltpu.VMEM((2, ROWS, IN_COLS), F32),
            pltpu.VMEM((2, ROWS, IN_COLS), F32),
            pltpu.VMEM(((SLOTS - 2) * ROWS, HEAD), F32),
            pltpu.VMEM((2 * ROWS, HEAD), F32),
            pltpu.VMEM(((SLOTS - 2) * ROWS, HEAD), F32),
            pltpu.VMEM((2, ROWS, OUT_ROWS), BF),
            pltpu.VMEM((NZ, 2, ROWS, OUT_ROWS), BF),
            pltpu.VMEM((NZ, 2, ROWS, IN_COLS), BF),
            pltpu.VMEM((NZ, 2, ROWS, IN_COLS), BF),
            pltpu.VMEM((2, ROWS, IN_COLS), BF),
            pltpu.VMEM((2, ROWS, IN_COLS), BF),
            pltpu.VMEM((NZ, ROWS, IN_COLS), BF),
            dma((2,)),
            dma((4,)), dma((4,)),
            dma((4,)), dma((4,)),
            dma((NZ,)), dma((NZ,)),
            dma((2,)), dma((2,)),
            dma((NZ,)), dma((NZ,)),
            dma((2,)), dma((2,)),
            dma((2,)), dma((2,)),
            dma((NZ,)), dma((NZ,)),
            dma((8,)), dma((8,)),
            dma((1,)), dma((1,)),
            dma((8,)), dma((8,)),
        ],
        compiler_params=pltpu.CompilerParams(collective_id=0, has_side_effects=True, vmem_limit_bytes=48 * 1024 * 1024),
    )(
        states, attn_gain[None], w_qkv, w_out, q_gain[None], k_gain[None], jnp.asarray(frequency), lengths,
        k_cache, v_cache,
    )


def solution(mesh):
    in_specs = (
        P(None, ("fsdp", "rep"), None),
        P(),
        P("fsdp", ("rep", "tp")),
        P(("rep", "tp"), "fsdp"),
        P(),
        P(),
        P(("fsdp", "rep"), "tp", None, None),
        P(("fsdp", "rep"), "tp", None, None),
        P(("fsdp", "rep")),
    )
    out_specs = P(None, ("fsdp", "rep"), None)
    return jax.shard_map(body, mesh=mesh, in_specs=in_specs, out_specs=out_specs, check_vma=False)
```

time: 381 us -> 75.5 us (0.20)
  waiting for transfers between devices: 322 us -> 0 us
  Pallas kernels: 0 us -> 64.9 us
  matrix products: 15.5 us -> 0 us
  local copies, waits for them, and re-layouts: 23.9 us -> 10.3 us
  between operations: 13.3 us -> 0.04 us
  other arithmetic: 5.26 us -> 0 us
    all_gather x4 -> x0, waiting for transfers between devices: 278 us -> none  [the longest x1 121 us: body(): lax.all_gather(own_in, 'fsdp', axis=0, tiled=True)]
    pallas_call x0 -> x1, Pallas kernels: none -> 64.9 us  [body(): pl.pallas_call(kernel, out_shape=jax.ShapeDtypeStruct(states.shape, BF),...]
    psum x1 -> x0, waiting for transfers between devices: 43.6 us -> none  [body(): summed = lax.psum(partial_out.astype(jnp.bfloat16), 'tp')]
    dot_general x1 -> x0, local copies, waits for them, and re-layouts: 17.7 us -> none  [body(): mixed = jnp.dot(normed, full_in, preferred_element_type=jnp.float32)]
    dot_general x6 -> x0, matrix products: 15.5 us -> none  [the longest x1 6.79 us: body(): mixed = jnp.dot(normed, full_in, preferred_element_type=jnp.float32)]
    unnamed x15 -> x18, local copies, waits for them, and re-layouts: 1.91 us -> 9.55 us
  transfers between devices with their start and end apart: 5 -> 0, of which waited for: 5 -> 0; matrix products, arithmetic and copies ran while one was open for 9% -> 0% of each run, Pallas kernels for 0% -> 0%
where the time goes in v1:
time: 75.5 us; the launch traced here: 75.2 us
  Pallas kernels  64.9 us (86%)
  local copies, waits for them, and re-layouts  10.3 us (14%)
    pallas_call x1, Pallas kernels, body(): pl.pallas_call(kernel, out_shape=jax.ShapeDtypeStruct(states.shape, BF),...  64.9 us
    unnamed x18, local copies, waits for them, and re-layouts  9.55 us

profile of v1, /device:TPU:1, one launch (start us, length us, event | category | flops | bytes accessed | tf_op | source)
XLA Modules:
  0.0 75.2 jit_solution(8056669941463097383)
XLA Ops:
  0.0 0.7 broadcast_in_dim.9.attn_gain
  0.7 1.2 %copy.11.w_out = f32[512,160]{1,0:T(8,128)S(1)} copy(f32[512,160]{0,1:T(8,128)} %param.13) | data formatting | bytes 655360 | tf_op args[3]
  1.9 0.0 copy-start
  1.9 1.6 %copy-done = bf16[4,1,2048,128]{3,2,1,0:T(8,128)(2,1)S(1)} copy-done((bf16[4,1,2048,128]{3,2,1,0:T(8,128)(2,1)S(1)}, bf16[4,1,2048,128]{3,2,1,0:T(8,128)(2,1)}, u32[]{:S(2)}) %copy-start) | copy-done | bytes 2097176
  3.5 0.0 copy-start.1
  3.5 1.6 %copy-done.1 = bf16[4,1,2048,128]{3,2,1,0:T(8,128)(2,1)S(1)} copy-done((bf16[4,1,2048,128]{3,2,1,0:T(8,128)(2,1)S(1)}, bf16[4,1,2048,128]{3,2,1,0:T(8,128)(2,1)}, u32[]{:S(2)}) %copy-start.1) | copy-done | bytes 2097176
  5.1 0.0 copy-start.2
  5.1 1.0 %copy-done.2 = f32[160,640]{1,0:T(8,128)S(1)} copy-done((f32[160,640]{1,0:T(8,128)S(1)}, f32[160,640]{1,0:T(8,128)}, u32[]{:S(2)}) %copy-start.2) | copy-done | bytes 409624
  6.1 0.0 copy-start.3
  6.1 0.9 %copy-done.3 = bf16[4,4,5120]{2,1,0:T(4,128)(2,1)S(1)} copy-done((bf16[4,4,5120]{2,1,0:T(4,128)(2,1)S(1)}, bf16[4,4,5120]{2,1,0:T(4,128)(2,1)}, u32[]{:S(2)}) %copy-start.3) | copy-done | bytes 163864
  7.0 0.0 copy-start.4
  7.0 0.7 copy-done.4
  7.7 0.0 copy-start.5
  7.7 0.7 copy-done.5
  8.3 0.0 copy-start.6
  8.3 0.7 copy-done.6
  9.0 0.0 copy-start.7
  9.0 0.7 copy-done.7
  9.6 64.9 %shard_map.100 = bf16[4,4,5120]{2,1,0:T(4,128)(2,1)S(1)} custom-call(bf16[4,4,5120]{2,1,0:T(4,128)(2,1)S(1)} %copy-done.3, bf16[1,5120]{1,0:T(2,128)(2,1)S(1)} %broadcast_in_dim.9.attn_gain, f32[160,640]{1,0:T(8,128)S(1)} %copy-done.2, f32[512,160]{1,0:T(8,128)S(1)} %copy.11.w_out, f32[1,128]{1,0:T(1,128)S(1)} %bitcast.2, f32[1,128]{1,0:T(1,128)S(1)} %bitcast.3, ...), custom_call_target="tpu_custom_call" | custom-call | tf_op jit(solution)/shard_map/pallas_call | solution.py:317
  74.5 0.7 copy.13
Async XLA Ops:
  1.9 1.6 %copy-start = (bf16[4,1,2048,128]{3,2,1,0:T(8,128)(2,1)S(1)}, bf16[4,1,2048,128]{3,2,1,0:T(8,128)(2,1)}, u32[]{:S(2)}) copy-start(bf16[4,1,2048,128]{3,2,1,0:T(8,128)(2,1)} %k_cache.1) | copy-start | bytes 6291460
  3.5 1.6 %copy-start.1 = (bf16[4,1,2048,128]{3,2,1,0:T(8,128)(2,1)S(1)}, bf16[4,1,2048,128]{3,2,1,0:T(8,128)(2,1)}, u32[]{:S(2)}) copy-start(bf16[4,1,2048,128]{3,2,1,0:T(8,128)(2,1)} %v_cache.1) | copy-start | bytes 6291460
  5.1 1.0 %copy-start.2 = (f32[160,640]{1,0:T(8,128)S(1)}, f32[160,640]{1,0:T(8,128)}, u32[]{:S(2)}) copy-start(f32[160,640]{1,0:T(8,128)} %w_qkv.1) | copy-start | bytes 1228804
  6.1 0.9 %copy-start.3 = (bf16[4,4,5120]{2,1,0:T(4,128)(2,1)S(1)}, bf16[4,4,5120]{2,1,0:T(4,128)(2,1)}, u32[]{:S(2)}) copy-start(bf16[4,4,5120]{2,1,0:T(4,128)(2,1)} %states.1) | copy-start | bytes 491524
  7.0 0.7 copy-start.4
  7.7 0.7 copy-start.5
  8.3 0.7 copy-start.6
  9.0 0.7 copy-start.7

commit v2 on v1

v2 whole, which is shorter than its diff:
```python
import functools
import math

import jax
import jax.numpy as jnp
import numpy as np
from jax import lax
from jax.experimental import pallas as pl
from jax.experimental.pallas import tpu as pltpu
from jax.sharding import PartitionSpec as P

MESH = pl.DeviceIdType.MESH
EPSILON = 1e-06
THETA = 1000000.0
NZ, NX = 8, 4
STEPS, SEQS, ROWS = 4, 4, 16
HEAD, SLOTS = 128, 10
IN_ROWS, IN_COLS = 160, 640
OUT_ROWS, OUT_COLS = 512, 160
CACHE, EXTRA = 2048, 128
KEYS = CACHE + EXTRA
BF, F32 = jnp.bfloat16, jnp.float32
O_AFTER = 5
O_PARTS = ((0, 80), (80, 80))
OUT_GROUPS = ((0, 4), (4, 4))
SUM_TYPE = jnp.bfloat16


def kernel(
    states_in, attn_gain_in, w_qkv_in, w_out_in, q_gain_in, k_gain_in, frequency_in, lengths_in, k_cache, v_cache, out,
    states, attn_gain, w_qkv, w_out, q_gain, k_gain, frequency, lengths,
    kbuf, vbuf, xs, nbuf, abuf, wbuf, obuf, cbuf, crecv, mrecv, qs, ks, cs, tbuf, xbuf, pbuf, precv, sbuf, rbuf, hbuf, ybuf,
    local_sem, w_send, w_recv, o_send, o_recv, a_send, a_recv, f_send, f_recv, c_send, c_recv,
    x_send, x_recv, p_send, p_recv, r_send, r_recv, h_send, h_recv,
):
    f, yl, tp = lax.axis_index("fsdp"), lax.axis_index("rep"), lax.axis_index("tp")
    z, x, yh, c = f // NX, f % NX, tp // 2, tp % 2
    y = yh * 2 + yl
    parity = z % 2
    toward = 1 - 2 * parity
    is_self = jnp.logical_and(yl == yh, yh == c)

    def at(pz, px, pl_, ph, pc):
        return (pz % NZ * NX + px % NX, pl_, ph * 2 + pc)

    def flip(d):
        return (1 - yl if d & 1 else yl, 1 - yh if d & 2 else yh, 1 - c if d & 4 else c)

    def send(src, dst, ssem, rsem, device):
        return pltpu.make_async_remote_copy(
            src_ref=src, dst_ref=dst, send_sem=ssem, recv_sem=rsem, device_id=device, device_id_type=MESH
        )

    other_core = at(z, x, yl, yh, 1 - c)
    sent = []

    def start(copy, when=None):
        sent.append((copy, when))
        if when is None:
            copy.start()
        else:
            pl.when(when)(copy.start)

    def wait(dst, rsem, when=None):
        arrival = send(dst, dst, h_send.at[0], rsem, other_core)
        if when is None:
            arrival.wait_recv()
        else:
            pl.when(when)(arrival.wait_recv)

    def finish():
        for copy, when in sent:
            if when is None:
                copy.wait_send()
            else:
                pl.when(when)(copy.wait_send)

    local = [
        (w_qkv_in, w_qkv),
        (states_in, states),
        (attn_gain_in, attn_gain),
        (lengths_in, lengths),
        (frequency_in, frequency),
        (w_out_in, w_out),
        (q_gain_in, q_gain),
        (k_gain_in, k_gain),
        (k_cache.at[:, 0], kbuf.at[:, pl.ds(0, CACHE)]),
        (v_cache.at[:, 0], vbuf.at[:, pl.ds(0, CACHE)]),
    ]
    local = [pltpu.make_async_copy(src, dst, local_sem.at[i]) for i, (src, dst) in enumerate(local)]
    for copy in local:
        copy.start()
    w_in, s_in, a_in, l_in, f_in, o_in, q_in, kg_in, k_copy, v_copy = local

    barrier = pltpu.get_barrier_semaphore()
    peers = [at(z, x + i, yl, yh, c) for i in range(1, NX)]
    peers += [at(z, x, *flip(d)) for d in range(1, 8)]
    peers += [at(z + c + 2 * i, x, 1 - yl, yh, c) for i in range(NZ // 2)]
    peers += [at(z + c + 2 * i, x, yl, yh, c) for i in range(1, NZ // 2)]
    peers += [at(z - m * toward + NZ, x, yl, yh, c) for m in range(1, 4)]
    for peer in peers:
        pl.semaphore_signal(barrier, inc=1, device_id=peer, device_id_type=MESH)

    @pl.when(c == 1)
    def _():
        pl.semaphore_signal(barrier, inc=1, device_id=at(z + 1, x, yl, yh, c), device_id_type=MESH)

    w_in.wait()
    wbuf[pl.ds(x, 1)] = w_qkv[...].astype(BF)[None]
    pl.semaphore_wait(barrier, len(peers) + c)

    right, left = at(z, x + 1, yl, yh, c), at(z, x + 3, yl, yh, c)
    rightward = ((0, 48), (48, 32), (80, 80))
    leftward = ((80, 48), (128, 32), (0, 80))

    def w_part(block, rows):
        return wbuf.at[block, pl.ds(*rows)]

    for n in range(3):
        start(send(w_part(x, rightward[n]), w_part(x, rightward[n]), w_send.at[0, n], w_recv.at[0, n], right))
        start(send(w_part(x, leftward[n]), w_part(x, leftward[n]), w_send.at[1, n], w_recv.at[1, n], left))

    s_in.wait()
    for s in range(STEPS):
        xs[pl.ds(s * SEQS, SEQS), :] = states[s].astype(F32)
    values = xs[...]
    mean = jnp.mean(values * values, axis=-1, keepdims=True)
    a_in.wait()
    normed = (values * lax.rsqrt(mean + EPSILON) * attn_gain[...].reshape(1, NZ * IN_COLS).astype(F32)).astype(BF)
    for k in range(NZ):
        nbuf[k] = normed[:, k * IN_COLS : (k + 1) * IN_COLS]

    @pl.when(c == 0)
    def _():
        abuf[0, pl.ds(yl, 1)] = nbuf[pl.ds(z, 1)]

    o_in.wait()
    obuf[0] = w_out[...].astype(BF)

    for i in (2, 1, 3, 0):
        k = c + 2 * i
        for rel in (0, 1):
            copy = send(
                nbuf.at[(z + k) % NZ], abuf.at[k, yl], a_send.at[i, rel], a_recv.at[i, rel],
                at(z + k, x, 1 - yl if rel else yl, yh, c),
            )
            start(copy, c == 1 if (i, rel) == (0, 0) else None)
    for copy in (l_in, f_in, q_in, kg_in):
        copy.wait()
    row = lax.broadcasted_iota(jnp.int32, (ROWS, HEAD), 0)
    lane = lax.broadcasted_iota(jnp.int32, (ROWS, HEAD), 1)
    position = row // SEQS
    for b in range(SEQS):
        position = position + jnp.where(row % SEQS == b, lengths[b], 0)
    angle = position.astype(F32) * frequency[...]
    cosine = jnp.cos(angle)
    sine = jnp.where(lane < HEAD // 2, -jnp.sin(angle), jnp.sin(angle))
    for b in range(SEQS):
        kbuf[b, pl.ds(CACHE, EXTRA), :] = jnp.zeros((EXTRA, HEAD), BF)
        vbuf[b, pl.ds(CACHE, EXTRA), :] = jnp.zeros((EXTRA, HEAD), BF)

    x_left, x_right, x_far = (x + 3) % NX, (x + 1) % NX, (x + 2) % NX

    def w_on(n):
        wait(w_part(x_left, rightward[n]), w_recv.at[0, n])
        start(send(w_part(x_left, rightward[n]), w_part(x_left, rightward[n]), w_send.at[2, n], w_recv.at[2, n], right))
        wait(w_part(x_right, leftward[n]), w_recv.at[1, n])
        start(send(w_part(x_right, leftward[n]), w_part(x_right, leftward[n]), w_send.at[3, n], w_recv.at[3, n], left))

    def send_back(n):
        rows = pl.ds(*O_PARTS[n])
        for m, ahead in ((3, -3), (2, 2), (1, -1)):
            target = at(z + ahead * toward + NZ, x, yl, yh, c)
            start(send(obuf.at[0, rows], obuf.at[m, rows], o_send.at[m, n], o_recv.at[m, n], target))

    w_on(0)
    for i in (0, 1, 3, 2):
        if i == 1:
            w_on(1)
        k = c + 2 * i
        for rel in (0, 1):
            wait(abuf.at[k, 1 - yl if rel else yl], a_recv.at[i, rel], c == 1 if (i, rel) == (0, 0) else None)
        start(send(abuf.at[k], abuf.at[k], f_send.at[i], f_recv.at[i], other_core))
    send_back(0)
    for i in range(NZ // 2):
        wait(abuf.at[1 - c + 2 * i], f_recv.at[i])
    wait(w_part(x_left, rightward[2]), w_recv.at[0, 2])
    wait(w_part(x_right, leftward[2]), w_recv.at[1, 2])
    for n in range(2):
        wait(w_part(x_far, rightward[n]), w_recv.at[2, n])
        wait(w_part(x_far, leftward[n]), w_recv.at[3, n])

    weights = wbuf[...].reshape(NX * IN_ROWS, IN_COLS)
    mixed = jnp.dot(abuf[...].reshape(NZ * 2 * ROWS, IN_COLS), weights, preferred_element_type=F32)
    cbuf[...] = mixed.reshape(NZ, 2, ROWS, IN_COLS).astype(SUM_TYPE)
    for k in (4, 3, 5, 2, 6, 1, 7, 0):
        for r in (0, 1):
            copy = send(cbuf.at[k, r], crecv.at[k, c], c_send.at[k, r], c_recv.at[k, c], at(z + NZ - k, x, r, yl, yh))
            start(copy, None if k else jnp.logical_not(jnp.logical_and(is_self, yl == r)))

    @pl.when(is_self)
    def _():
        crecv[0, pl.ds(c, 1)] = cbuf[0, pl.ds(yl, 1)]

    for k in (0, 1, 7, 2, 6, 3, 5, 4):
        for cc in (0, 1):
            wait(crecv.at[k, cc], c_recv.at[k, cc], None if k else jnp.logical_not(jnp.logical_and(is_self, c == cc)))
        if k == O_AFTER:
            send_back(1)
    for cc in (0, 1):
        total = crecv[0, cc].astype(F32)
        for k in range(1, NZ):
            total = total + crecv[k, cc].astype(F32)
        mrecv[cc] = total

    def slot(j):
        at_half = SLOTS // 2
        return mrecv[j // at_half, :, pl.ds((j % at_half) * HEAD, HEAD)]

    def roped(v, gain):
        n = v * lax.rsqrt(jnp.mean(v * v, axis=-1, keepdims=True) + EPSILON) * gain
        return (n * cosine + pltpu.roll(n, HEAD // 2, 1) * sine).astype(BF).astype(F32)

    for j in range(SLOTS - 2):
        qs[pl.ds(j * ROWS, ROWS), :] = roped(slot(j), q_gain[...])
    ks[pl.ds(0, ROWS), :] = roped(slot(SLOTS - 2), k_gain[...])
    ks[pl.ds(ROWS, ROWS), :] = slot(SLOTS - 1)
    k_copy.wait()
    v_copy.wait()
    queries_of = STEPS * (SLOTS - 2)
    scale = 1.0 / math.sqrt(HEAD)
    column = lax.broadcasted_iota(jnp.int32, (queries_of, KEYS), 1)
    step = lax.broadcasted_iota(jnp.int32, (queries_of, KEYS), 0) % STEPS
    new_valid = jnp.logical_and(column >= CACHE, column - CACHE <= step)
    for b in range(SEQS):
        query = qs[pl.ds(b, queries_of, stride=SEQS), :].astype(BF)
        empty = jnp.zeros((ROWS - STEPS, HEAD), F32)
        kbuf[b, pl.ds(CACHE, ROWS), :] = jnp.concatenate([ks[pl.ds(b, STEPS, stride=SEQS), :], empty], axis=0).astype(BF)
        vbuf[b, pl.ds(CACHE, ROWS), :] = jnp.concatenate([ks[pl.ds(ROWS + b, STEPS, stride=SEQS), :], empty], axis=0).astype(BF)
        scores = lax.dot_general(query, kbuf[b], (((1,), (1,)), ((), ())), preferred_element_type=F32) * scale
        valid = jnp.logical_or(column < lengths[b], new_valid)
        highest = jnp.max(jnp.where(valid, scores, -1e30), axis=-1, keepdims=True)
        exps = jnp.where(valid, jnp.exp(scores - highest), 0.0)
        probs = (exps / jnp.sum(exps, axis=-1, keepdims=True)).astype(BF)
        cs[pl.ds(b, queries_of, stride=SEQS), :] = jnp.dot(probs, vbuf[b], preferred_element_type=F32)
    per_half = (SLOTS - 2) // 2
    for j in range(SLOTS - 2):
        tbuf[j // per_half, :, pl.ds((j % per_half) * HEAD, HEAD)] = cs[pl.ds(j * ROWS, ROWS), :].astype(BF)

    order = (0, 1, 3, 4, 2, 5, 7, 6)

    def place(q, *rest):
        return at(z + q // NX * toward, x + q % NX, *rest)

    for q in reversed(order):
        back = order.index(q // NX * NX + (NX - q) % NX)
        for cc in (0, 1):
            copy = send(tbuf.at[cc], xbuf.at[back, yl], x_send.at[q, cc], x_recv.at[back, yl], place(q, yh, c, cc))
            start(copy, None if q else jnp.logical_not(jnp.logical_and(is_self, c == cc)))

    @pl.when(is_self)
    def _():
        xbuf[0, pl.ds(yl, 1)] = tbuf[pl.ds(c, 1)]

    for m in range(1, 4):
        for n in range(2):
            wait(obuf.at[m, pl.ds(*O_PARTS[n])], o_recv.at[m, n])
    back_weights = obuf[...].reshape(4 * OUT_COLS, OUT_ROWS)
    own_sum = jnp.logical_and(parity == c, c == yl)

    def multiply(first, count):
        for n in range(first, first + count):
            for r in (0, 1):
                wait(xbuf.at[n, r], x_recv.at[n, r], None if n else jnp.logical_not(jnp.logical_and(is_self, yl == r)))
        rows = xbuf[pl.ds(first, count)].reshape(count * 2 * ROWS, OUT_ROWS)
        partial = lax.dot_general(rows, back_weights, (((1,), (1,)), ((), ())), preferred_element_type=F32)
        pbuf[pl.ds(first, count)] = partial.reshape(count, 2, ROWS, 4 * OUT_COLS)
        for n in range(first, first + count):
            start(send(pbuf.at[n, 1 - c], precv.at[n], p_send.at[n], p_recv.at[n], other_core))

    def pass_on(n):
        wait(precv.at[n], p_recv.at[n])
        sbuf[n] = (pbuf[n, c] + precv[n]).astype(BF)
        for hh in (0, 1):
            copy = send(sbuf.at[n], rbuf.at[x, y], r_send.at[n, hh], r_recv.at[x, y], place(order[n], c, hh, parity))
            start(copy, None if n else jnp.logical_not(jnp.logical_and(own_sum, yh == hh)))

    for first, count in OUT_GROUPS:
        multiply(first, count)
        for n in range(first, first + count):
            pass_on(n)

    @pl.when(own_sum)
    def _():
        rbuf[pl.ds(x, 1), pl.ds(y, 1)] = sbuf[0][None, None]

    for xx in range(NX):
        for yy in range(4):
            here = jnp.logical_and(own_sum, jnp.logical_and(x == xx, y == yy))
            wait(rbuf.at[xx, yy], r_recv.at[xx, yy], jnp.logical_not(here))
        total = rbuf[xx, 0].astype(F32)
        for yy in range(1, 4):
            total = total + rbuf[xx, yy].astype(F32)
        hbuf[pl.ds(c, 1), xx] = total.astype(BF)[None]
        start(send(hbuf.at[c, xx], hbuf.at[c, xx], h_send.at[xx], h_recv.at[xx], other_core))
    def assemble(side):
        blocks = [hbuf[pl.ds(side, 1), xx].astype(F32)[0] for xx in range(NX)]
        for m in range(4):
            wide = jnp.concatenate([block[:, m * OUT_COLS : (m + 1) * OUT_COLS] for block in blocks], axis=1)
            ybuf[pl.ds((z - parity + side + (2 * side - 1) * m + NZ) % NZ, 1)] = wide[None]

    assemble(c)
    for xx in range(NX):
        wait(hbuf.at[1 - c, xx], h_recv.at[xx])
    assemble(1 - c)
    for k in range(NZ):
        block_rows = ybuf[k]
        for s in range(STEPS):
            out[s, :, pl.ds(k * IN_COLS, IN_COLS)] = block_rows[s * SEQS : (s + 1) * SEQS].astype(BF)
    finish()


def body(states, attn_gain, w_qkv, w_out, q_gain, k_gain, k_cache, v_cache, lengths):
    half = HEAD // 2
    exponent = np.arange(half, dtype=np.float64) * (-math.log(THETA) / half)
    frequency = np.tile(np.exp(exponent).astype(np.float32), 2)[None]
    width = states.shape[2]
    vmem, hbm = pl.BlockSpec(memory_space=pltpu.VMEM), pl.BlockSpec(memory_space=pltpu.HBM)
    dma = pltpu.SemaphoreType.DMA
    return pl.pallas_call(
        kernel,
        out_shape=jax.ShapeDtypeStruct(states.shape, BF),
        in_specs=[hbm] * 10,
        out_specs=vmem,
        scratch_shapes=[
            pltpu.VMEM(states.shape, BF),
            pltpu.VMEM(attn_gain.shape, BF),
            pltpu.VMEM(w_qkv.shape, F32),
            pltpu.VMEM((OUT_COLS, OUT_ROWS), F32),
            pltpu.VMEM((1, HEAD), F32),
            pltpu.VMEM((1, HEAD), F32),
            pltpu.VMEM((1, HEAD), F32),
            pltpu.SMEM((SEQS,), jnp.int32),
            pltpu.VMEM((SEQS, KEYS, HEAD), BF),
            pltpu.VMEM((SEQS, KEYS, HEAD), BF),
            pltpu.VMEM((ROWS, width), F32),
            pltpu.VMEM((NZ, ROWS, IN_COLS), BF),
            pltpu.VMEM((NZ, 2, ROWS, IN_COLS), BF),
            pltpu.VMEM((NX, IN_ROWS, IN_COLS), BF),
            pltpu.VMEM((4, OUT_COLS, OUT_ROWS), BF),
            pltpu.VMEM((NZ, 2, ROWS, IN_COLS), SUM_TYPE),
            pltpu.VMEM((NZ, 2, ROWS, IN_COLS), SUM_TYPE),
            pltpu.VMEM((2, ROWS, IN_COLS), F32),
            pltpu.VMEM(((SLOTS - 2) * ROWS, HEAD), F32),
            pltpu.VMEM((2 * ROWS, HEAD), F32),
            pltpu.VMEM(((SLOTS - 2) * ROWS, HEAD), F32),
            pltpu.VMEM((2, ROWS, OUT_ROWS), BF),
            pltpu.VMEM((8, 2, ROWS, OUT_ROWS), BF),
            pltpu.VMEM((8, 2, ROWS, IN_COLS), F32),
            pltpu.VMEM((8, ROWS, IN_COLS), F32),
            pltpu.VMEM((8, ROWS, IN_COLS), BF),
            pltpu.VMEM((NX, 4, ROWS, IN_COLS), BF),
            pltpu.VMEM((2, NX, ROWS, IN_COLS), BF),
            pltpu.VMEM((NZ, ROWS, IN_COLS), F32),
            dma((10,)),
            dma((4, 3)), dma((4, 3)),
            dma((4, 2)), dma((4, 2)),
            dma((4, 2)), dma((4, 2)),
            dma((4,)), dma((4,)),
            dma((NZ, 2)), dma((NZ, 2)),
            dma((8, 2)), dma((8, 2)),
            dma((8,)), dma((8,)),
            dma((8, 2)), dma((NX, 4)),
            dma((NX,)), dma((NX,)),
        ],
        compiler_params=pltpu.CompilerParams(collective_id=0, has_side_effects=True, vmem_limit_bytes=63 * 1024 * 1024),
    )(
        states, attn_gain, w_qkv, w_out.T, q_gain[None], k_gain[None], jnp.asarray(frequency), lengths,
        k_cache, v_cache,
    )


def solution(mesh):
    in_specs = (
        P(None, ("fsdp", "rep"), None),
        P(),
        P("fsdp", ("rep", "tp")),
        P(("rep", "tp"), "fsdp"),
        P(),
        P(),
        P(("fsdp", "rep"), "tp", None, None),
        P(("fsdp", "rep"), "tp", None, None),
        P(("fsdp", "rep")),
    )
    out_specs = P(None, ("fsdp", "rep"), None)
    return jax.shard_map(body, mesh=mesh, in_specs=in_specs, out_specs=out_specs, check_vma=False)
```

time: 75.5 us -> 56.9 us (0.75)
  Pallas kernels: 64.9 us -> 55.1 us
  local copies, waits for them, and re-layouts: 10.3 us -> 1.64 us
    pallas_call x1, Pallas kernels: 64.9 us -> 55.1 us  [body(): pl.pallas_call(kernel, out_shape=jax.ShapeDtypeStruct(states.shape, BF),...]
    unnamed x18 -> x1, local copies, waits for them, and re-layouts: 9.55 us -> 1.64 us
where the time goes in v2:
time: 56.9 us; the launch traced here: 56.8 us
  Pallas kernels  55.1 us (97%)
  local copies, waits for them, and re-layouts  1.64 us (3%)
    pallas_call x1, Pallas kernels, body(): pl.pallas_call(kernel, out_shape=jax.ShapeDtypeStruct(states.shape, BF),...  55.1 us
    unnamed x1, local copies, waits for them, and re-layouts  1.64 us

profile of v2, /device:TPU:1, one launch (start us, length us, event | category | flops | bytes accessed | tf_op | source)
XLA Modules:
  0.0 56.8 jit_solution(16309760941470191163)
XLA Ops:
  0.0 55.1 %shard_map.100 = bf16[4,4,5120]{2,1,0:T(4,128)(2,1)} custom-call(bf16[4,4,5120]{2,1,0:T(4,128)(2,1)} %states_in.1, bf16[5120]{0:T(1024)(128)(2,1)} %attn_gain_in.1, f32[160,640]{1,0:T(8,128)} %w_qkv_in.1, f32[160,512]{1,0:T(8,128)} %bitcast.3, f32[1,128]{1,0:T(1,128)} %bitcast.4, f32[1,128]{1,0:T(1,128)} %bitcast.5, f32[1,128]{1,0:T(1,128)} %constant.2.clone.frequency_in, ...), custom_call_target="tpu_custom_call" | custom-call | tf_op jit(solution)/shard_map/pallas_call | solution.py:330
  55.2 1.6 %copy.12 = bf16[4,4,5120]{2,1,0:T(4,128)(2,1)} copy(bf16[4,4,5120]{2,1,0:T(4,128)(2,1)} %shard_map.100) | data formatting | bytes 327680

commit v3 on v2

--- a/solution.py
+++ b/solution.py
@@ -21,7 +21,7 @@
 KEYS = CACHE + EXTRA
 BF, F32 = jnp.bfloat16, jnp.float32
 O_AFTER = 5
-O_PARTS = ((0, 80), (80, 80))
+O_FIRST, O_SECOND = 0, 0
 OUT_GROUPS = ((0, 4), (4, 4))
 SUM_TYPE = jnp.bfloat16
 
@@ -29,9 +29,9 @@
 def kernel(
     states_in, attn_gain_in, w_qkv_in, w_out_in, q_gain_in, k_gain_in, frequency_in, lengths_in, k_cache, v_cache, out,
     states, attn_gain, w_qkv, w_out, q_gain, k_gain, frequency, lengths,
-    kbuf, vbuf, xs, nbuf, abuf, wbuf, obuf, cbuf, crecv, mrecv, qs, ks, cs, tbuf, xbuf, pbuf, precv, sbuf, rbuf, hbuf, ybuf,
+    kbuf, vbuf, xs, nbuf, abuf, wbuf, obuf, cbuf, crecv, mrecv, qs, ks, cs, tbuf, xbuf, sbuf, rbuf, hbuf, ybuf,
     local_sem, w_send, w_recv, o_send, o_recv, a_send, a_recv, f_send, f_recv, c_send, c_recv,
-    x_send, x_recv, p_send, p_recv, r_send, r_recv, h_send, h_recv,
+    x_send, x_recv, q_send, q_recv, r_send, r_recv, h_send, h_recv,
 ):
     f, yl, tp = lax.axis_index("fsdp"), lax.axis_index("rep"), lax.axis_index("tp")
     z, x, yh, c = f // NX, f % NX, tp // 2, tp % 2
@@ -74,6 +74,19 @@
                 copy.wait_send()
             else:
                 pl.when(when)(copy.wait_send)
+
+    barrier = pltpu.get_barrier_semaphore()
+    peers = [at(z, x + i, yl, yh, c) for i in range(1, NX)]
+    peers += [at(z, x, *flip(d)) for d in range(1, 8)]
+    peers += [at(z + c + 2 * i, x, 1 - yl, yh, c) for i in range(NZ // 2)]
+    peers += [at(z + c + 2 * i, x, yl, yh, c) for i in range(1, NZ // 2)]
+    peers += [at(z - m * toward + NZ, x, yl, yh, c) for m in range(1, 3)]
+    for peer in peers:
+        pl.semaphore_signal(barrier, inc=1, device_id=peer, device_id_type=MESH)
+
+    @pl.when(c == 1)
+    def _():
+        pl.semaphore_signal(barrier, inc=1, device_id=at(z + 1, x, yl, yh, c), device_id_type=MESH)
 
     local = [
         (w_qkv_in, w_qkv),
@@ -92,34 +105,8 @@
         copy.start()
     w_in, s_in, a_in, l_in, f_in, o_in, q_in, kg_in, k_copy, v_copy = local
 
-    barrier = pltpu.get_barrier_semaphore()
-    peers = [at(z, x + i, yl, yh, c) for i in range(1, NX)]
-    peers += [at(z, x, *flip(d)) for d in range(1, 8)]
-    peers += [at(z + c + 2 * i, x, 1 - yl, yh, c) for i in range(NZ // 2)]
-    peers += [at(z + c + 2 * i, x, yl, yh, c) for i in range(1, NZ // 2)]
-    peers += [at(z - m * toward + NZ, x, yl, yh, c) for m in range(1, 4)]
-    for peer in peers:
-        pl.semaphore_signal(barrier, inc=1, device_id=peer, device_id_type=MESH)
-
-    @pl.when(c == 1)
-    def _():
-        pl.semaphore_signal(barrier, inc=1, device_id=at(z + 1, x, yl, yh, c), device_id_type=MESH)
-
     w_in.wait()
     wbuf[pl.ds(x, 1)] = w_qkv[...].astype(BF)[None]
-    pl.semaphore_wait(barrier, len(peers) + c)
-
-    right, left = at(z, x + 1, yl, yh, c), at(z, x + 3, yl, yh, c)
-    rightward = ((0, 48), (48, 32), (80, 80))
-    leftward = ((80, 48), (128, 32), (0, 80))
-
-    def w_part(block, rows):
-        return wbuf.at[block, pl.ds(*rows)]
-
-    for n in range(3):
-        start(send(w_part(x, rightward[n]), w_part(x, rightward[n]), w_send.at[0, n], w_recv.at[0, n], right))
-        start(send(w_part(x, leftward[n]), w_part(x, leftward[n]), w_send.at[1, n], w_recv.at[1, n], left))
-
     s_in.wait()
     for s in range(STEPS):
         xs[pl.ds(s * SEQS, SEQS), :] = states[s].astype(F32)
@@ -135,7 +122,20 @@
         abuf[0, pl.ds(yl, 1)] = nbuf[pl.ds(z, 1)]
 
     o_in.wait()
-    obuf[0] = w_out[...].astype(BF)
+    obuf[pl.ds(c, 1), 0] = w_out[...].astype(BF)[None]
+
+    pl.semaphore_wait(barrier, len(peers) + c)
+
+    right, left = at(z, x + 1, yl, yh, c), at(z, x + 3, yl, yh, c)
+    rightward = ((0, 48), (48, 32), (80, 80))
+    leftward = ((80, 48), (128, 32), (0, 80))
+
+    def w_part(block, rows):
+        return wbuf.at[block, pl.ds(*rows)]
+
+    for n in range(3):
+        start(send(w_part(x, rightward[n]), w_part(x, rightward[n]), w_send.at[0, n], w_recv.at[0, n], right))
+        start(send(w_part(x, leftward[n]), w_part(x, leftward[n]), w_send.at[1, n], w_recv.at[1, n], left))
 
     for i in (2, 1, 3, 0):
         k = c + 2 * i
@@ -167,21 +167,26 @@
         wait(w_part(x_right, leftward[n]), w_recv.at[1, n])
         start(send(w_part(x_right, leftward[n]), w_part(x_right, leftward[n]), w_send.at[3, n], w_recv.at[3, n], left))
 
-    def send_back(n):
-        rows = pl.ds(*O_PARTS[n])
-        for m, ahead in ((3, -3), (2, 2), (1, -1)):
-            target = at(z + ahead * toward + NZ, x, yl, yh, c)
-            start(send(obuf.at[0, rows], obuf.at[m, rows], o_send.at[m, n], o_recv.at[m, n], target))
+    def send_back(block, slot, ahead):
+        target = at(z + ahead * toward + NZ, x, yl, yh, c)
+        start(send(obuf.at[c, block], obuf.at[c, slot], o_send.at[slot], o_recv.at[slot], target))
+
+    def share_back(slot):
+        start(send(obuf.at[c, slot], obuf.at[c, slot], q_send.at[slot], q_recv.at[slot], other_core))
 
     w_on(0)
-    for i in (0, 1, 3, 2):
-        if i == 1:
+    for n, i in enumerate((0, 1, 3, 2)):
+        if n == 1:
             w_on(1)
         k = c + 2 * i
         for rel in (0, 1):
             wait(abuf.at[k, 1 - yl if rel else yl], a_recv.at[i, rel], c == 1 if (i, rel) == (0, 0) else None)
         start(send(abuf.at[k], abuf.at[k], f_send.at[i], f_recv.at[i], other_core))
-    send_back(0)
+        if n == O_FIRST:
+            send_back(0, 1, -1)
+        if n == O_SECOND:
+            send_back(0, 2, 2)
+    share_back(0)
     for i in range(NZ // 2):
         wait(abuf.at[1 - c + 2 * i], f_recv.at[i])
     wait(w_part(x_left, rightward[2]), w_recv.at[0, 2])
@@ -206,7 +211,11 @@
         for cc in (0, 1):
             wait(crecv.at[k, cc], c_recv.at[k, cc], None if k else jnp.logical_not(jnp.logical_and(is_self, c == cc)))
         if k == O_AFTER:
-            send_back(1)
+            wait(obuf.at[c, 1], o_recv.at[1])
+            send_back(1, 3, 2)
+            share_back(1)
+    wait(obuf.at[c, 2], o_recv.at[2])
+    share_back(2)
     for cc in (0, 1):
         total = crecv[0, cc].astype(F32)
         for k in range(1, NZ):
@@ -254,41 +263,34 @@
 
     for q in reversed(order):
         back = order.index(q // NX * NX + (NX - q) % NX)
-        for cc in (0, 1):
-            copy = send(tbuf.at[cc], xbuf.at[back, yl], x_send.at[q, cc], x_recv.at[back, yl], place(q, yh, c, cc))
-            start(copy, None if q else jnp.logical_not(jnp.logical_and(is_self, c == cc)))
+        copy = send(tbuf, xbuf.at[back], x_send.at[q], x_recv.at[back], place(q, yh, c, yl))
+        start(copy, None if q else jnp.logical_not(is_self))
 
     @pl.when(is_self)
     def _():
-        xbuf[0, pl.ds(yl, 1)] = tbuf[pl.ds(c, 1)]
-
-    for m in range(1, 4):
-        for n in range(2):
-            wait(obuf.at[m, pl.ds(*O_PARTS[n])], o_recv.at[m, n])
-    back_weights = obuf[...].reshape(4 * OUT_COLS, OUT_ROWS)
+        xbuf[0] = tbuf[...]
+
+    wait(obuf.at[c, 3], o_recv.at[3])
+    share_back(3)
+    for m in range(4):
+        wait(obuf.at[1 - c, m], q_recv.at[m])
+    back_weights = [obuf[half].reshape(4 * OUT_COLS, OUT_ROWS) for half in (0, 1)]
     own_sum = jnp.logical_and(parity == c, c == yl)
-
-    def multiply(first, count):
+    for first, count in OUT_GROUPS:
         for n in range(first, first + count):
-            for r in (0, 1):
-                wait(xbuf.at[n, r], x_recv.at[n, r], None if n else jnp.logical_not(jnp.logical_and(is_self, yl == r)))
-        rows = xbuf[pl.ds(first, count)].reshape(count * 2 * ROWS, OUT_ROWS)
-        partial = lax.dot_general(rows, back_weights, (((1,), (1,)), ((), ())), preferred_element_type=F32)
-        pbuf[pl.ds(first, count)] = partial.reshape(count, 2, ROWS, 4 * OUT_COLS)
-        for n in range(first, first + count):
-            start(send(pbuf.at[n, 1 - c], precv.at[n], p_send.at[n], p_recv.at[n], other_core))
-
-    def pass_on(n):
-        wait(precv.at[n], p_recv.at[n])
-        sbuf[n] = (pbuf[n, c] + precv[n]).astype(BF)
-        for hh in (0, 1):
-            copy = send(sbuf.at[n], rbuf.at[x, y], r_send.at[n, hh], r_recv.at[x, y], place(order[n], c, hh, parity))
-            start(copy, None if n else jnp.logical_not(jnp.logical_and(own_sum, yh == hh)))
-
-    for first, count in OUT_GROUPS:
-        multiply(first, count)
-        for n in range(first, first + count):
-            pass_on(n)
+            wait(xbuf.at[n], x_recv.at[n], None if n else jnp.logical_not(is_self))
+        partial = sum(
+            lax.dot_general(
+                xbuf[pl.ds(first, count), half].reshape(count * ROWS, OUT_ROWS), back_weights[half],
+                (((1,), (1,)), ((), ())), preferred_element_type=F32,
+            )
+            for half in (0, 1)
+        )
+        sbuf[pl.ds(first, count)] = partial.reshape(count, ROWS, 4 * OUT_COLS).astype(BF)
+        for n in reversed(range(first, first + count)):
+            for hh in (0, 1):
+                copy = send(sbuf.at[n], rbuf.at[x, y], r_send.at[n, hh], r_recv.at[x, y], place(order[n], c, hh, parity))
+                start(copy, None if n else jnp.logical_not(jnp.logical_and(own_sum, yh == hh)))
 
     @pl.when(own_sum)
     def _():
@@ -325,13 +327,12 @@
     exponent = np.arange(half, dtype=np.float64) * (-math.log(THETA) / half)
     frequency = np.tile(np.exp(exponent).astype(np.float32), 2)[None]
     width = states.shape[2]
-    vmem, hbm = pl.BlockSpec(memory_space=pltpu.VMEM), pl.BlockSpec(memory_space=pltpu.HBM)
+    hbm = pl.BlockSpec(memory_space=pltpu.HBM)
     dma = pltpu.SemaphoreType.DMA
     return pl.pallas_call(
         kernel,
-        out_shape=jax.ShapeDtypeStruct(states.shape, BF),
+        out_shape=pltpu.VMEM(states.shape, BF),
         in_specs=[hbm] * 10,
-        out_specs=vmem,
         scratch_shapes=[
             pltpu.VMEM(states.shape, BF),
             pltpu.VMEM(attn_gain.shape, BF),
@@ -347,7 +348,7 @@
             pltpu.VMEM((NZ, ROWS, IN_COLS), BF),
             pltpu.VMEM((NZ, 2, ROWS, IN_COLS), BF),
             pltpu.VMEM((NX, IN_ROWS, IN_COLS), BF),
-            pltpu.VMEM((4, OUT_COLS, OUT_ROWS), BF),
+            pltpu.VMEM((2, 4, OUT_COLS, OUT_ROWS), BF),
             pltpu.VMEM((NZ, 2, ROWS, IN_COLS), SUM_TYPE),
             pltpu.VMEM((NZ, 2, ROWS, IN_COLS), SUM_TYPE),
             pltpu.VMEM((2, ROWS, IN_COLS), F32),
@@ -356,20 +357,18 @@
             pltpu.VMEM(((SLOTS - 2) * ROWS, HEAD), F32),
             pltpu.VMEM((2, ROWS, OUT_ROWS), BF),
             pltpu.VMEM((8, 2, ROWS, OUT_ROWS), BF),
-            pltpu.VMEM((8, 2, ROWS, IN_COLS), F32),
-            pltpu.VMEM((8, ROWS, IN_COLS), F32),
             pltpu.VMEM((8, ROWS, IN_COLS), BF),
             pltpu.VMEM((NX, 4, ROWS, IN_COLS), BF),
             pltpu.VMEM((2, NX, ROWS, IN_COLS), BF),
             pltpu.VMEM((NZ, ROWS, IN_COLS), F32),
             dma((10,)),
             dma((4, 3)), dma((4, 3)),
-            dma((4, 2)), dma((4, 2)),
+            dma((4,)), dma((4,)),
             dma((4, 2)), dma((4, 2)),
             dma((4,)), dma((4,)),
             dma((NZ, 2)), dma((NZ, 2)),
-            dma((8, 2)), dma((8, 2)),
             dma((8,)), dma((8,)),
+            dma((4,)), dma((4,)),
             dma((8, 2)), dma((NX, 4)),
             dma((NX,)), dma((NX,)),
         ],

time: 56.9 us -> 51.5 us (0.905)
  Pallas kernels: 55.1 us -> 50.7 us
  local copies, waits for them, and re-layouts: 1.64 us -> 0.67 us
    pallas_call x1, Pallas kernels: 55.1 us -> 50.7 us  [body(): pl.pallas_call(kernel, out_shape=pltpu.VMEM(states.shape, BF), in_specs=[...]
    unnamed x1, local copies, waits for them, and re-layouts: 1.64 us -> 0.67 us
where the time goes in v3:
time: 51.5 us; the launch traced here: 51.4 us
  Pallas kernels  50.7 us (98%)
  local copies, waits for them, and re-layouts  0.67 us (1%)
    pallas_call x1, Pallas kernels, body(): pl.pallas_call(kernel, out_shape=pltpu.VMEM(states.shape, BF), in_specs=[...  50.7 us

profile of v3, /device:TPU:1, one launch (start us, length us, event | category | flops | bytes accessed | tf_op | source)
XLA Modules:
  0.0 51.4 jit_solution(4844512000559135521)
XLA Ops:
  0.0 50.7 %shard_map.100 = bf16[4,4,5120]{2,1,0:T(4,128)(2,1)S(1)} custom-call(bf16[4,4,5120]{2,1,0:T(4,128)(2,1)} %states_in.1, bf16[5120]{0:T(1024)(128)(2,1)} %attn_gain_in.1, f32[160,640]{1,0:T(8,128)} %w_qkv_in.1, f32[160,512]{1,0:T(8,128)} %bitcast.3, f32[1,128]{1,0:T(1,128)} %bitcast.4, f32[1,128]{1,0:T(1,128)} %bitcast.5, ...), custom_call_target="tpu_custom_call" | custom-call | tf_op jit(solution)/shard_map/pallas_call | solution.py:332
  50.7 0.7 %copy.12 = bf16[4,4,5120]{2,1,0:T(4,128)(2,1)} copy(bf16[4,4,5120]{2,1,0:T(4,128)(2,1)S(1)} %shard_map.100) | data formatting | bytes 327680

commit v4 on v3

--- a/solution.py
+++ b/solution.py
@@ -21,7 +21,7 @@
 KEYS = CACHE + EXTRA
 BF, F32 = jnp.bfloat16, jnp.float32
 O_AFTER = 5
-O_FIRST, O_SECOND = 0, 0
+O_EARLY = 80
 OUT_GROUPS = ((0, 4), (4, 4))
 SUM_TYPE = jnp.bfloat16
 
@@ -167,9 +167,12 @@
         wait(w_part(x_right, leftward[n]), w_recv.at[1, n])
         start(send(w_part(x_right, leftward[n]), w_part(x_right, leftward[n]), w_send.at[3, n], w_recv.at[3, n], left))
 
-    def send_back(block, slot, ahead):
+    early, late = pl.ds(0, O_EARLY), pl.ds(O_EARLY, OUT_COLS - O_EARLY)
+
+    def send_back(block, slot, ahead, rows=pl.ds(0, OUT_COLS), n=None):
         target = at(z + ahead * toward + NZ, x, yl, yh, c)
-        start(send(obuf.at[c, block], obuf.at[c, slot], o_send.at[slot], o_recv.at[slot], target))
+        n = slot if n is None else n
+        start(send(obuf.at[c, block, rows], obuf.at[c, slot, rows], o_send.at[n], o_recv.at[n], target))
 
     def share_back(slot):
         start(send(obuf.at[c, slot], obuf.at[c, slot], q_send.at[slot], q_recv.at[slot], other_core))
@@ -182,10 +185,9 @@
         for rel in (0, 1):
             wait(abuf.at[k, 1 - yl if rel else yl], a_recv.at[i, rel], c == 1 if (i, rel) == (0, 0) else None)
         start(send(abuf.at[k], abuf.at[k], f_send.at[i], f_recv.at[i], other_core))
-        if n == O_FIRST:
+        if n == 0:
             send_back(0, 1, -1)
-        if n == O_SECOND:
-            send_back(0, 2, 2)
+            send_back(0, 2, 2, early)
     share_back(0)
     for i in range(NZ // 2):
         wait(abuf.at[1 - c + 2 * i], f_recv.at[i])
@@ -196,12 +198,22 @@
         wait(w_part(x_far, leftward[n]), w_recv.at[3, n])
 
     weights = wbuf[...].reshape(NX * IN_ROWS, IN_COLS)
-    mixed = jnp.dot(abuf[...].reshape(NZ * 2 * ROWS, IN_COLS), weights, preferred_element_type=F32)
-    cbuf[...] = mixed.reshape(NZ, 2, ROWS, IN_COLS).astype(SUM_TYPE)
-    for k in (4, 3, 5, 2, 6, 1, 7, 0):
-        for r in (0, 1):
-            copy = send(cbuf.at[k, r], crecv.at[k, c], c_send.at[k, r], c_recv.at[k, c], at(z + NZ - k, x, r, yl, yh))
-            start(copy, None if k else jnp.logical_not(jnp.logical_and(is_self, yl == r)))
+    for part in ((4, 3, 5, 2), (6, 1, 7, 0)):
+        if 0 in part:
+            rows = jnp.concatenate([abuf[pl.ds(6, 2)], abuf[pl.ds(0, 2)]], axis=0)
+        else:
+            rows = abuf[pl.ds(2, 4)]
+        mixed = jnp.dot(rows.reshape(NZ * ROWS, IN_COLS), weights, preferred_element_type=F32)
+        mixed = mixed.reshape(NZ // 2, 2, ROWS, IN_COLS).astype(SUM_TYPE)
+        if 0 in part:
+            cbuf[pl.ds(6, 2)] = mixed[:2]
+            cbuf[pl.ds(0, 2)] = mixed[2:]
+        else:
+            cbuf[pl.ds(2, 4)] = mixed
+        for k in part:
+            for r in (0, 1):
+                copy = send(cbuf.at[k, r], crecv.at[k, c], c_send.at[k, r], c_recv.at[k, c], at(z + NZ - k, x, r, yl, yh))
+                start(copy, None if k else jnp.logical_not(jnp.logical_and(is_self, yl == r)))
 
     @pl.when(is_self)
     def _():
@@ -211,11 +223,10 @@
         for cc in (0, 1):
             wait(crecv.at[k, cc], c_recv.at[k, cc], None if k else jnp.logical_not(jnp.logical_and(is_self, c == cc)))
         if k == O_AFTER:
+            send_back(0, 2, 2, late, 0)
             wait(obuf.at[c, 1], o_recv.at[1])
             send_back(1, 3, 2)
             share_back(1)
-    wait(obuf.at[c, 2], o_recv.at[2])
-    share_back(2)
     for cc in (0, 1):
         total = crecv[0, cc].astype(F32)
         for k in range(1, NZ):
@@ -237,7 +248,7 @@
     k_copy.wait()
     v_copy.wait()
     queries_of = STEPS * (SLOTS - 2)
-    scale = 1.0 / math.sqrt(HEAD)
+    scale = math.log2(math.e) / math.sqrt(HEAD)
     column = lax.broadcasted_iota(jnp.int32, (queries_of, KEYS), 1)
     step = lax.broadcasted_iota(jnp.int32, (queries_of, KEYS), 0) % STEPS
     new_valid = jnp.logical_and(column >= CACHE, column - CACHE <= step)
@@ -246,11 +257,11 @@
         empty = jnp.zeros((ROWS - STEPS, HEAD), F32)
         kbuf[b, pl.ds(CACHE, ROWS), :] = jnp.concatenate([ks[pl.ds(b, STEPS, stride=SEQS), :], empty], axis=0).astype(BF)
         vbuf[b, pl.ds(CACHE, ROWS), :] = jnp.concatenate([ks[pl.ds(ROWS + b, STEPS, stride=SEQS), :], empty], axis=0).astype(BF)
-        scores = lax.dot_general(query, kbuf[b], (((1,), (1,)), ((), ())), preferred_element_type=F32) * scale
+        scores = lax.dot_general(query, kbuf[b], (((1,), (1,)), ((), ())), preferred_element_type=F32)
         valid = jnp.logical_or(column < lengths[b], new_valid)
-        highest = jnp.max(jnp.where(valid, scores, -1e30), axis=-1, keepdims=True)
-        exps = jnp.where(valid, jnp.exp(scores - highest), 0.0)
-        probs = (exps / jnp.sum(exps, axis=-1, keepdims=True)).astype(BF)
+        scores = jnp.where(valid, scores, -1e30)
+        exps = jnp.exp2((scores - jnp.max(scores, axis=-1, keepdims=True)) * scale)
+        probs = (exps * (1.0 / jnp.sum(exps, axis=-1, keepdims=True))).astype(BF)
         cs[pl.ds(b, queries_of, stride=SEQS), :] = jnp.dot(probs, vbuf[b], preferred_element_type=F32)
     per_half = (SLOTS - 2) // 2
     for j in range(SLOTS - 2):
@@ -270,6 +281,9 @@
     def _():
         xbuf[0] = tbuf[...]
 
+    wait(obuf.at[c, 2, early], o_recv.at[2])
+    wait(obuf.at[c, 2, late], o_recv.at[0])
+    share_back(2)
     wait(obuf.at[c, 3], o_recv.at[3])
     share_back(3)
     for m in range(4):

time: 51.5 us -> 50.7 us (0.984)
  Pallas kernels: 50.7 us -> 49.9 us
    pallas_call x1, Pallas kernels: 50.7 us -> 49.9 us  [body(): pl.pallas_call(kernel, out_shape=pltpu.VMEM(states.shape, BF), in_specs=[...]
where the time goes in v4:
time: 50.7 us; the launch traced here: 50.6 us
  Pallas kernels  49.9 us (98%)
  local copies, waits for them, and re-layouts  0.67 us (1%)
    pallas_call x1, Pallas kernels, body(): pl.pallas_call(kernel, out_shape=pltpu.VMEM(states.shape, BF), in_specs=[...  49.9 us

profile of v4, /device:TPU:1, one launch (start us, length us, event | category | flops | bytes accessed | tf_op | source)
XLA Modules:
  0.0 50.6 jit_solution(1977288456528804205)
XLA Ops:
  0.0 49.9 %shard_map.100 = bf16[4,4,5120]{2,1,0:T(4,128)(2,1)S(1)} custom-call(bf16[4,4,5120]{2,1,0:T(4,128)(2,1)} %states_in.1, bf16[5120]{0:T(1024)(128)(2,1)} %attn_gain_in.1, f32[160,640]{1,0:T(8,128)} %w_qkv_in.1, f32[160,512]{1,0:T(8,128)} %bitcast.3, f32[1,128]{1,0:T(1,128)} %bitcast.4, f32[1,128]{1,0:T(1,128)} %bitcast.5, ...), custom_call_target="tpu_custom_call" | custom-call | tf_op jit(solution)/shard_map/pallas_call | solution.py:346
  49.9 0.7 %copy.12 = bf16[4,4,5120]{2,1,0:T(4,128)(2,1)} copy(bf16[4,4,5120]{2,1,0:T(4,128)(2,1)S(1)} %shard_map.100) | data formatting | bytes 327680

commit v5 on v4

--- a/solution.py
+++ b/solution.py
@@ -68,12 +68,14 @@
         else:
             pl.when(when)(arrival.wait_recv)
 
-    def finish():
-        for copy, when in sent:
+    def finish(keep=0):
+        done = len(sent) - keep
+        for copy, when in sent[:done]:
             if when is None:
                 copy.wait_send()
             else:
                 pl.when(when)(copy.wait_send)
+        del sent[:done]
 
     barrier = pltpu.get_barrier_semaphore()
     peers = [at(z, x + i, yl, yh, c) for i in range(1, NX)]
@@ -101,7 +103,7 @@
         (v_cache.at[:, 0], vbuf.at[:, pl.ds(0, CACHE)]),
     ]
     local = [pltpu.make_async_copy(src, dst, local_sem.at[i]) for i, (src, dst) in enumerate(local)]
-    for copy in local:
+    for copy in local[:3] + local[8:]:
         copy.start()
     w_in, s_in, a_in, l_in, f_in, o_in, q_in, kg_in, k_copy, v_copy = local
 
@@ -121,8 +123,8 @@
     def _():
         abuf[0, pl.ds(yl, 1)] = nbuf[pl.ds(z, 1)]
 
-    o_in.wait()
-    obuf[pl.ds(c, 1), 0] = w_out[...].astype(BF)[None]
+    for copy in local[3:8]:
+        copy.start()
 
     pl.semaphore_wait(barrier, len(peers) + c)
 
@@ -145,6 +147,8 @@
                 at(z + k, x, 1 - yl if rel else yl, yh, c),
             )
             start(copy, c == 1 if (i, rel) == (0, 0) else None)
+    o_in.wait()
+    obuf[pl.ds(c, 1), 0] = w_out[...].astype(BF)[None]
     for copy in (l_in, f_in, q_in, kg_in):
         copy.wait()
     row = lax.broadcasted_iota(jnp.int32, (ROWS, HEAD), 0)
@@ -219,19 +223,18 @@
     def _():
         crecv[0, pl.ds(c, 1)] = cbuf[0, pl.ds(yl, 1)]
 
+    total = [jnp.zeros((ROWS, IN_COLS), F32)] * 2
     for k in (0, 1, 7, 2, 6, 3, 5, 4):
         for cc in (0, 1):
             wait(crecv.at[k, cc], c_recv.at[k, cc], None if k else jnp.logical_not(jnp.logical_and(is_self, c == cc)))
+            total[cc] = total[cc] + crecv[k, cc].astype(F32)
         if k == O_AFTER:
             send_back(0, 2, 2, late, 0)
             wait(obuf.at[c, 1], o_recv.at[1])
             send_back(1, 3, 2)
             share_back(1)
     for cc in (0, 1):
-        total = crecv[0, cc].astype(F32)
-        for k in range(1, NZ):
-            total = total + crecv[k, cc].astype(F32)
-        mrecv[cc] = total
+        mrecv[cc] = total[cc]
 
     def slot(j):
         at_half = SLOTS // 2
@@ -281,6 +284,7 @@
     def _():
         xbuf[0] = tbuf[...]
 
+    finish(len(order))
     wait(obuf.at[c, 2, early], o_recv.at[2])
     wait(obuf.at[c, 2, late], o_recv.at[0])
     share_back(2)
@@ -305,6 +309,8 @@
             for hh in (0, 1):
                 copy = send(sbuf.at[n], rbuf.at[x, y], r_send.at[n, hh], r_recv.at[x, y], place(order[n], c, hh, parity))
                 start(copy, None if n else jnp.logical_not(jnp.logical_and(own_sum, yh == hh)))
+
+    finish(2 * len(order))
 
     @pl.when(own_sum)
     def _():

time: 50.7 us -> 50.7 us (level)
  no operation moved by 1% of the time
where the time goes in v5:
time: 50.7 us; the launch traced here: 50.6 us
  Pallas kernels  49.9 us (98%)
  local copies, waits for them, and re-layouts  0.67 us (1%)
    pallas_call x1, Pallas kernels, body(): pl.pallas_call(kernel, out_shape=pltpu.VMEM(states.shape, BF), in_specs=[...  49.9 us

profile of v5, /device:TPU:1, one launch (start us, length us, event | category | flops | bytes accessed | tf_op | source)
XLA Modules:
  0.0 50.6 jit_solution(16836051441328224787)
XLA Ops:
  0.0 49.9 %shard_map.100 = bf16[4,4,5120]{2,1,0:T(4,128)(2,1)S(1)} custom-call(bf16[4,4,5120]{2,1,0:T(4,128)(2,1)} %states_in.1, bf16[5120]{0:T(1024)(128)(2,1)} %attn_gain_in.1, f32[160,640]{1,0:T(8,128)} %w_qkv_in.1, f32[160,512]{1,0:T(8,128)} %bitcast.3, f32[1,128]{1,0:T(1,128)} %bitcast.4, f32[1,128]{1,0:T(1,128)} %bitcast.5, ...), custom_call_target="tpu_custom_call" | custom-call | tf_op jit(solution)/shard_map/pallas_call | solution.py:352
  49.9 0.7 %copy.12 = bf16[4,4,5120]{2,1,0:T(4,128)(2,1)} copy(bf16[4,4,5120]{2,1,0:T(4,128)(2,1)S(1)} %shard_map.100) | data formatting | bytes 327680
